TPU v7x, 32 devices: a whole 2x2x4 slice. The times are simulated.
32 devices in a mesh: panel: 8 (over y, x, core), slab: 4 (over z).
Axes of the slice: x: 2, y: 2, z: 4, core: 2. Of those that a mesh axis runs over, the one named last changes fastest.
Arguments:
- clip_cache: float32 [1024, 1024], P(None, 'panel'), may hold values from -6 to 6
- dose_scale: float32 [16, 1024], P(None, 'panel'), may hold values from 0.3 to 3
- focus_term: float32 [8, 1024], P(None, 'panel'), may hold values from -3 to 3
- clip_ids: int32 [32768], P('slab'), may hold values from 0 to 1023
- dose_ids: int32 [32768], P('slab'), may hold values from 0 to 15
- focus_ids: int32 [32768], P('slab'), may hold values from 0 to 7
Outputs:
- rotated: float32 [32768, 1024], P('slab', 'panel')
All inputs are finite; a program needn't handle non-finite values.
Results may differ from a plain program's by a relative error of at most 0.0001.
Values sent between devices are 32-bit elements; how exact they have to be, the bound alone decides.
No kernel may reach another device: no remote copies, remote signals or barrier semaphores. Data moves between devices by JAX's collectives and lax.ppermute only.
A program may use at most 64 MiB of HBM per device.

v0:
```python
import jax
import jax.numpy as jnp
from jax import lax
from jax.sharding import PartitionSpec as P

ROUNDS = 2


EPSILON = 1e-06


def from_behind(block, axis, distance):
    devices = range(lax.axis_size(axis))
    route = [((i - distance) % len(devices), i) for i in devices]
    return lax.ppermute(block, axis, route)


def from_partner(value, axis, distance):
    mask = 2**distance
    pairs = [(source, source ^ mask) for source in range(lax.axis_size(axis))]
    return lax.ppermute(value, axis, pairs)


def block_rotation(gram):
    doubled = gram.shape[0]
    half_size = doubled // 2
    diagonal = jnp.diagonal(gram)
    coupling = gram / (diagonal[:, None] + diagonal[None, :])
    positions = lax.iota(jnp.int32, doubled)
    upper_mask = (positions[:, None] < half_size) & (positions[None, :] >= half_size)
    lower_mask = (positions[:, None] >= half_size) & (positions[None, :] < half_size)
    generator = 0.5 * (jnp.where(upper_mask, coupling, 0.0) - jnp.where(lower_mask, coupling, 0.0))
    identity = jnp.eye(doubled, dtype=gram.dtype)
    plus_half = identity + generator
    symmetric = identity + jnp.dot(
        generator.T, generator, precision=lax.Precision.HIGHEST, preferred_element_type=jnp.float32
    )
    factor = jnp.linalg.cholesky(symmetric)
    numerator = jnp.dot(
        plus_half, plus_half, precision=lax.Precision.HIGHEST, preferred_element_type=jnp.float32
    )
    return jax.scipy.linalg.cho_solve((factor, True), numerator)


def lookup(table_rows, indices):
    positions = lax.iota(jnp.int32, table_rows.shape[0])
    one_hot = (positions[:, None] == indices[None, :]).astype(jnp.float32)
    return lax.dot_general(
        one_hot,
        table_rows,
        (((0,), (0,)), ((), ())),
        precision=lax.Precision.HIGHEST,
        preferred_element_type=jnp.float32,
    )


def slab_gram(pair_block):
    gram_local = lax.dot_general(
        pair_block,
        pair_block,
        (((0,), (0,)), ((), ())),
        precision=lax.Precision.HIGHEST,
        preferred_element_type=jnp.float32,
    )
    return lax.psum(gram_local, "slab")


def product(left_side, right_side):
    return jnp.dot(
        left_side, right_side, precision=lax.Precision.HIGHEST, preferred_element_type=jnp.float32
    )


def shards(clip_cache, dose_scale, focus_term, clip_ids, dose_ids, focus_ids):
    row_count = clip_ids.shape[0]
    total_rows = row_count * lax.axis_size("slab")
    panel_width = clip_cache.shape[1]
    dose_part = lookup(dose_scale, dose_ids)
    focus_part = lookup(focus_term, focus_ids)
    jacobian = jnp.take(clip_cache, clip_ids, axis=0) * dose_part + focus_part
    col_squares = lax.psum(jnp.sum(jacobian * jacobian, axis=0), "slab")
    jacobian = jacobian * (1.0 / jnp.sqrt(col_squares / total_rows + EPSILON))
    seat_index = lax.axis_index("panel")
    is_odd = seat_index % 2 == 1
    own_start = seat_index % 2 * panel_width
    current = jacobian
    for section in range(ROUNDS):
        if section > 0:
            current = from_behind(current, "panel", 1)
        partner = from_partner(current, "panel", 0)
        pair_block = jnp.where(
            is_odd,
            jnp.concatenate([partner, current], axis=1),
            jnp.concatenate([current, partner], axis=1),
        )
        rotation = block_rotation(slab_gram(pair_block))
        own_cols = lax.dynamic_slice_in_dim(rotation, own_start, panel_width, 1)
        current = product(pair_block, own_cols)
    return current


def solution(mesh):
    return jax.shard_map(
        shards,
        mesh=mesh,
        in_specs=(
            P(None, "panel"),
            P(None, "panel"),
            P(None, "panel"),
            P("slab"),
            P("slab"),
            P("slab"),
        ),
        out_specs=P("slab", "panel"),
        check_vma=False,
    )
```

profile of v0, /device:TPU:0, one launch (start us, length us, event | category | flops | bytes accessed | tf_op | source)
XLA Modules:
  0.0 402.1 jit_solution(4020237490650624477)
XLA Ops:
  8.2 28.0 %gather_fusion = f32[8192,128]{1,0:T(8,128)} fusion(f32[1024,128]{1,0:T(8,128)S(1)} %copy-done, s32[8192]{0:T(1024)S(1)} %fusion.42), kind=kCustom, calls=%fused_computation | custom fusion | bytes 8421376 | tf_op jit(solution)/shard_map/jit(_take)/gather | solution.py:80
  36.1 5.7 %copy.15 = f32[8192,128]{0,1:T(8,128)} copy(f32[8192,128]{1,0:T(8,128)} %gather_fusion) | data formatting | bytes 8388608 | tf_op jit(solution)/shard_map/jit(_take)/gather | solution.py:80
  41.8 4.2 %convolution_multiply_fusion = f32[8192,128]{0,1:T(8,128)S(1)} fusion(f32[16,128]{1,0:T(8,128)S(1)} %copy-done.5, f32[8192,128]{0,1:T(8,128)} %copy.15, pred[8192]{0:T(1024)(128)(4,1)S(1)} %compare_and_fusion, s32[8192]{0:T(1024)S(1)} %copy-done.3), kind=kOutput, calls=%fused_computation.8 | convolution fusion | flops 203554816 | bytes 8437760 | tf_op jit(solution)/shard_map/dot_general | solution.py:48
  46.0 4.2 %multiply_reduce_fusion = (f32[128]{0:T(128)S(1)}, f32[8192,128]{0,1:T(8,128)}) fusion(f32[8192,128]{0,1:T(8,128)S(1)} %convolution_multiply_fusion, f32[8,128]{1,0:T(8,128)S(1)} %copy-done.6, s32[8192]{0:T(1024)S(1)} %copy-done.4), kind=kOutput, calls=%fused_computation.15 | convolution fusion | flops 103874432 | bytes 8425984 | tf_op jit(solution)/shard_map/dot_general | solution.py:48
  50.2 13.4 %psum.21 = f32[128]{0:T(128)S(1)} all-reduce(f32[128]{0:T(128)S(1)} %get-tuple-element.51), channel_id=1, replica_groups=mesh['panel'=8,'slab'=4] {'slab'}, use_global_device_ids=true, to_apply=%region_1.2 | all-reduce | flops 128 | bytes 1024 | tf_op jit(solution)/shard_map/psum | solution.py:81
  63.6 4.7 %broadcast_multiply_fusion = f32[8192,128]{0,1:T(8,128)} fusion(f32[8192,128]{0,1:T(8,128)} %get-tuple-element.52, f32[128]{0:T(128)S(1)} %add_rsqrt_fusion), kind=kLoop, calls=%fused_computation.20 | loop fusion | flops 1048576 | bytes 8389120 | tf_op jit(solution)/shard_map/mul | solution.py:82
  68.3 7.5 %collective-permute-done = f32[8192,128]{0,1:T(8,128)} collective-permute-done((f32[8192,128]{0,1:T(8,128)}, f32[8192,128]{0,1:T(8,128)}, u32[]{:S(2)}, u32[]{:S(2)}) %collective-permute-start) | collective-permute-done | bytes 4194336 | tf_op jit(solution)/shard_map/ppermute | solution.py:21
  75.8 15.8 %fusion.3 = f32[256,256]{0,1:T(8,128)} fusion(f32[8192,128]{0,1:T(8,128)} %broadcast_multiply_fusion, f32[8192,128]{0,1:T(8,128)} %collective-permute-done, pred[]{:T(512)S(6)} %eq.42), kind=kOutput, calls=%fused_computation.14 | convolution fusion | flops 6448742400 | bytes 8650753 | tf_op jit(solution)/shard_map/dot_general | solution.py:58
  92.2 33.1 %all-reduce.4.cloned.1.call-done = f32[256,256]{0,1:T(8,128)} async-done(((f32[256,256]{0,1:T(8,128)}), f32[256,256]{0,1:T(8,128)}) %all-reduce.4.cloned.1.call-update) | async-done | bytes 262160 | tf_op jit(solution)/shard_map/psum | solution.py:65
  129.8 11.7 %cholesky.130 = f32[128,128]{1,0:T(8,128)S(1)} custom-call(f32[128,128]{1,0:T(8,128)S(1)} %cholesky.194), custom_call_target="Cholesky" | custom-call | tf_op jit(solution)/shard_map/jit(cholesky)/cholesky | solution.py:38
  141.6 9.8 %custom-call.19 = f32[1,128,128]{1,2,0:T(8,128)S(1)} custom-call(f32[1,128,128]{2,1,0:T(8,128)S(1)} %get-tuple-element.50), custom_call_target="InvertDiagBlocksLowerTriangular" | custom-call | tf_op jit(solution)/shard_map/jit(cholesky)/cholesky | solution.py:38
  151.9 11.7 %cholesky.147 = f32[128,128]{1,0:T(8,128)S(1)} custom-call(f32[128,128]{1,0:T(8,128)S(1)} %convolution_subtract_fusion.5), custom_call_target="Cholesky" | custom-call | tf_op jit(solution)/shard_map/jit(cholesky)/cholesky | solution.py:38
  166.4 4.1 %while.4 = (s32[]{:T(128)}, f32[256,256]{1,0:T(8,128)S(1)}, s32[2,2]{1,0:T(2,128)S(1)}, f32[2,128,128]{2,1,0:T(8,128)S(1)}, s32[]{:T(128)}) while((s32[]{:T(128)}, f32[256,256]{1,0:T(8,128)S(1)}, s32[2,2]{1,0:T(2,128)S(1)}, f32[2,128,128]{2,1,0:T(8,128)S(1)}, s32[]{:T(128)}) %tuple.44), condition=%wide.while_cond, body=%wide.while_body.sunk | while | flops 2 | bytes 131181 | solution.py:42
  170.5 19.7 %custom-call.20 = f32[2,128,128]{1,2,0:T(8,128)S(1)} custom-call(f32[2,128,128]{2,1,0:T(8,128)S(1)} %get-tuple-element.21), custom_call_target="InvertDiagBlocksLowerTriangular" | custom-call | tf_op jit(solution)/shard_map/jit(_cho_solve)/triangular_solve | solution.py:42
  192.8 8.8 %fusion.2 = f32[8192,128]{0,1:T(8,128)S(1)} fusion(f32[8192,128]{0,1:T(8,128)} %broadcast_multiply_fusion, f32[8192,128]{0,1:T(8,128)} %collective-permute-done, pred[]{:T(512)S(6)} %eq.42, s32[]{:T(128)S(6)} %select_n.63, f32[128,256]{1,0:T(8,128)S(1)} %fusion.32, f32[128,256]{1,0:T(8,128)S(1)} %fusion.33), kind=kOutput, calls=%fused_computation.13 | convolution fusion | flops 3227549696 | bytes 12845061 | tf_op jit(solution)/shard_map/dot_general | solution.py:69
  201.7 48.8 %collective-permute-done.1 = f32[8192,128]{0,1:T(8,128)S(1)} collective-permute-done((f32[8192,128]{0,1:T(8,128)S(1)}, f32[8192,128]{0,1:T(8,128)S(1)}, u32[]{:S(2)}, u32[]{:S(2)}) %collective-permute-start.1) | collective-permute-done | bytes 4194336 | tf_op jit(solution)/shard_map/ppermute | solution.py:15
  252.4 7.3 %collective-permute-done.2 = f32[8192,128]{0,1:T(8,128)} collective-permute-done((f32[8192,128]{0,1:T(8,128)S(1)}, f32[8192,128]{0,1:T(8,128)}, u32[]{:S(2)}, u32[]{:S(2)}) %collective-permute-start.2) | collective-permute-done | bytes 4194336 | tf_op jit(solution)/shard_map/ppermute | solution.py:21
  259.7 15.2 %fusion.1 = f32[256,256]{0,1:T(8,128)} fusion(f32[8192,128]{0,1:T(8,128)} %copy-done.7, f32[8192,128]{0,1:T(8,128)} %collective-permute-done.2, pred[]{:T(512)S(6)} %eq.42), kind=kOutput, calls=%fused_computation.12 | convolution fusion | flops 6448742400 | bytes 8650753 | tf_op jit(solution)/shard_map/dot_general | solution.py:58
  275.0 34.3 %all-reduce.6.cloned.1.call-done = f32[256,256]{0,1:T(8,128)} async-done(((f32[256,256]{0,1:T(8,128)}), f32[256,256]{0,1:T(8,128)}) %all-reduce.6.cloned.1.call-update) | async-done | bytes 262160 | tf_op jit(solution)/shard_map/psum | solution.py:65
  313.8 11.7 %cholesky.164 = f32[128,128]{1,0:T(8,128)S(1)} custom-call(f32[128,128]{1,0:T(8,128)S(1)} %cholesky.197), custom_call_target="Cholesky" | custom-call | tf_op jit(solution)/shard_map/jit(cholesky)/cholesky | solution.py:38
  325.6 9.8 %custom-call.21 = f32[1,128,128]{1,2,0:T(8,128)S(1)} custom-call(f32[1,128,128]{2,1,0:T(8,128)S(1)} %get-tuple-element.46), custom_call_target="InvertDiagBlocksLowerTriangular" | custom-call | tf_op jit(solution)/shard_map/jit(cholesky)/cholesky | solution.py:38
  335.9 11.7 %cholesky.181 = f32[128,128]{1,0:T(8,128)S(1)} custom-call(f32[128,128]{1,0:T(8,128)S(1)} %convolution_subtract_fusion.4), custom_call_target="Cholesky" | custom-call | tf_op jit(solution)/shard_map/jit(cholesky)/cholesky | solution.py:38
  354.0 19.9 %custom-call.22 = f32[2,128,128]{1,2,0:T(8,128)S(1)} custom-call(f32[2,128,128]{2,1,0:T(8,128)S(1)} %get-tuple-element.22), custom_call_target="InvertDiagBlocksLowerTriangular" | custom-call | tf_op jit(solution)/shard_map/jit(_cho_solve)/triangular_solve | solution.py:42
  376.6 18.2 %fusion = f32[8192,128]{1,0:T(8,128)} fusion(f32[8192,128]{0,1:T(8,128)} %copy-done.7, f32[8192,128]{0,1:T(8,128)} %collective-permute-done.2, pred[]{:T(512)S(6)} %eq.42, s32[]{:T(128)S(6)} %select_n.63, f32[128,256]{1,0:T(8,128)S(1)} %fusion.35, f32[128,256]{1,0:T(8,128)S(1)} %fusion.36), kind=kOutput, calls=%fused_computation.11 | convolution fusion | flops 3227549696 | bytes 12845061 | tf_op jit(solution)/shard_map/dot_general | solution.py:69
  (85 shorter events, 33.7 us)
Async XLA Ops:
  6.5 1.6 copy-start
  6.5 118.8 %all-reduce.4.cloned.1.call-start = ((), (), s32[]{:S(2)}) async-start(), calls=%async_computation | async-start | bytes 524288 | tf_op jit(solution)/shard_map/psum | solution.py:65
  36.1 5.7 %copy-start.3 = (s32[8192]{0:T(1024)S(1)}, s32[8192]{0:T(1024)}, u32[]{:S(2)}) copy-start(s32[8192]{0:T(1024)} %param.13) | copy-start | bytes 98308
  36.1 5.7 %copy-start.5 = (f32[16,128]{1,0:T(8,128)S(1)}, f32[16,128]{1,0:T(8,128)}, u32[]{:S(2)}) copy-start(f32[16,128]{1,0:T(8,128)} %param.10) | copy-start | bytes 24580
  41.8 4.2 %copy-start.4 = (s32[8192]{0:T(1024)S(1)}, s32[8192]{0:T(1024)}, u32[]{:S(2)}) copy-start(s32[8192]{0:T(1024)} %param.14) | copy-start | bytes 98308
  41.8 4.2 %copy-start.6 = (f32[8,128]{1,0:T(8,128)S(1)}, f32[8,128]{1,0:T(8,128)}, u32[]{:S(2)}) copy-start(f32[8,128]{1,0:T(8,128)} %param.11) | copy-start | bytes 12292
  68.3 7.5 %collective-permute-start = (f32[8192,128]{0,1:T(8,128)}, f32[8192,128]{0,1:T(8,128)}, u32[]{:S(2)}, u32[]{:S(2)}) collective-permute-start(f32[8192,128]{0,1:T(8,128)} %broadcast_multiply_fusion), channel_id=1, source_target_pairs={{0,4},{4,0},{8,12},{12,8},{16,20},{20,16},{24,28},{28,24},{1,5},{5... | collective-permute-start | bytes 12582920 | tf_op jit(solution)/shard_map/ppermute | solution.py:21
  91.6 217.7 %all-reduce.6.cloned.1.call-start = ((), (), s32[]{:S(2)}) async-start(), calls=%async_computation.1 | async-start | bytes 524288 | tf_op jit(solution)/shard_map/psum | solution.py:65
  125.3 64.9 %copy-start.1 = (f32[256,256]{0,1:T(8,128)S(1)}, f32[256,256]{0,1:T(8,128)}, u32[]{:S(2)}) copy-start(f32[256,256]{0,1:T(8,128)} %all-reduce.4.cloned.1.call-done) | copy-start | bytes 786436
  201.6 48.9 %collective-permute-start.1 = (f32[8192,128]{0,1:T(8,128)S(1)}, f32[8192,128]{0,1:T(8,128)S(1)}, u32[]{:S(2)}, u32[]{:S(2)}) collective-permute-start(f32[8192,128]{0,1:T(8,128)S(1)} %fusion.2), channel_id=1, source_target_pairs={{28,0},{0,4},{4,8},{8,12},{12,16},{16,20},{20,24},{24,28},{29,1},{... | collective-permute-start | bytes 12582920 | tf_op jit(solution)/shard_map/ppermute | solution.py:15
  250.5 1.9 copy-start.7
  252.4 7.3 %collective-permute-start.2 = (f32[8192,128]{0,1:T(8,128)S(1)}, f32[8192,128]{0,1:T(8,128)}, u32[]{:S(2)}, u32[]{:S(2)}) collective-permute-start(f32[8192,128]{0,1:T(8,128)S(1)} %collective-permute-done.1), channel_id=1, source_target_pairs={{0,4},{4,0},{8,12},{12,8},{16,20},{20,16},{24,28},{28,24},{1,5},{5... | collective-permute-start | bytes 12582920 | tf_op jit(solution)/shard_map/ppermute | solution.py:21
  309.3 64.7 %copy-start.2 = (f32[256,256]{0,1:T(8,128)S(1)}, f32[256,256]{0,1:T(8,128)}, u32[]{:S(2)}) copy-start(f32[256,256]{0,1:T(8,128)} %all-reduce.6.cloned.1.call-done) | copy-start | bytes 786436
Sparse Core Ops, SparseCore 0:
  91.7 33.5 all-reduce.3
  275.1 34.1 all-reduce.5
where the time goes:
time: 408 us; the launch traced here: 402 us
  waiting for transfers between devices  131 us (32%)
  other arithmetic  115 us (28%)
  matrix products  75.7 us (19%)
  local copies, waits for them, and re-layouts  49 us (12%)
  between operations  16.7 us (4%)
  blocking collectives  13.4 us (3%)
    another operation x14, other arithmetic, block_rotation(): factor = jnp.linalg.cholesky(symmetric)  69.2 us
    psum x2, waiting for transfers between devices, slab_gram(): return lax.psum(gram_local, 'slab')  67.5 us
    ppermute x1, waiting for transfers between devices, from_behind(): return lax.ppermute(block, axis, route)  48.8 us
    another operation x5, other arithmetic, block_rotation(): return jax.scipy.linalg.cho_solve((factor, True), numerator)  39.7 us
    gather x2, local copies, waits for them, and re-layouts, shards(): jacobian = jnp.take(clip_cache, clip_ids, axis=0) * dose_part + focus_part  33.6 us
    dot_general x2, matrix products, slab_gram(): lax.dot_general(pair_block, pair_block, (((0,), (0,)), ((), ())), precisi...  31 us
    dot_general x2, matrix products, product(): jnp.dot(left_side, right_side, precision=lax.Precision.HIGHEST, preferred...  27 us
    ppermute x2, waiting for transfers between devices, from_partner(): return lax.ppermute(value, axis, pairs)  14.8 us
  transfers between devices with their start and end apart: 5, of which 5 were waited for; matrix products, arithmetic and copies ran while one was open for 0% of the time, Pallas kernels for 0%

commit v1 on v0

v1 whole, which is shorter than its diff:
```python
import jax
import jax.numpy as jnp
from jax import lax
from jax.experimental import pallas as pl
from jax.experimental.pallas import tpu as pltpu
from jax.sharding import PartitionSpec as P

EPSILON = 1e-06
VMEM_LIMIT = 48 * 2**20
HIGHEST = lax.Precision.HIGHEST
COUNT_PARTS = 2
MARGIN = 8
BRIEF = pl.CostEstimate(flops=1, bytes_accessed=1, transcendentals=0)


def from_partner(value):
    count = lax.axis_size("panel")
    return lax.ppermute(value, "panel", [(i, i ^ 1) for i in range(count)])


def from_previous_pair(value):
    count = lax.axis_size("panel")
    return lax.ppermute(value, "panel", [(i, (i + 2) % count) for i in range(count)])


def from_other_slabs(value):
    slabs = lax.axis_size("slab")
    paired = slabs & (slabs - 1) == 0
    target = lambda i, d: i ^ d if paired else (i + d) % slabs
    return [
        lax.ppermute(value, "slab", [(i, target(i, d)) for i in range(slabs)])
        for d in range(1, slabs)
    ]


def split(value):
    high = value.astype(jnp.bfloat16)
    low = (value - high.astype(jnp.float32)).astype(jnp.bfloat16)
    return high, low


def bdot(left, right, dims=((1,), (0,))):
    return lax.dot_general(left, right, (dims, ((), ())), preferred_element_type=jnp.float32)


def split3(value):
    high, rest = split(value)
    middle = value - high.astype(jnp.float32)
    low = (middle - rest.astype(jnp.float32)).astype(jnp.bfloat16)
    return high, rest, low


def dot3(left, right):
    (a, b), (c, d) = split(left), split(right)
    return bdot(jnp.concatenate([a, b, a], axis=1), jnp.concatenate([c, c, d], axis=0))


def dot6(left, right):
    (a, b, c), (d, e, f) = split3(left), split3(right)
    lefts, rights = [a, a, b, b, a, c], [d, e, d, e, f, d]
    return bdot(jnp.concatenate(lefts, axis=1), jnp.concatenate(rights, axis=0))


def fdot(left, right, dims=((1,), (0,))):
    return lax.dot_general(
        left, right, (dims, ((), ())), precision=HIGHEST, preferred_element_type=jnp.float32
    )


def layout_kernel(odd_ref, clips, doses, focuses, *refs):
    id_refs, (table, ids, own, pairs), spaces, sems = refs[:3], refs[3:7], refs[7:10], refs[10]
    start = 0
    copies = []
    for k, ref in enumerate((clips, doses, focuses)):
        part = table.at[pl.ds(start, ref.shape[0])]
        copies.append(pltpu.make_async_copy(ref, part, sems.at[k]))
        start += ref.shape[0]
    for k, (ref, space) in enumerate(zip(id_refs, spaces)):
        copies.append(pltpu.make_async_copy(ref, space, sems.at[3 + k]))
    for copy in copies:
        copy.start()
    half = own.shape[1]
    begin = pl.multiple_of(odd_ref[0] * half, half)
    for k, space in enumerate(spaces):
        copies[3 + k].wait()
        ids[k : k + 1, :] = space[...]
        own[k : k + 1, :] = space[:, pl.ds(begin, half)]
    pairs[...] = ids[1:2, :] * clips.shape[0] + ids[0:1, :]
    for copy in copies[:3]:
        copy.wait()


def layout(odd, clip_cache, dose_scale, focus_term, *ids):
    rows = clip_cache.shape[0] + dose_scale.shape[0] + focus_term.shape[0]
    count = ids[0].shape[0]
    return pl.pallas_call(
        layout_kernel,
        in_specs=[pl.BlockSpec(memory_space=pltpu.SMEM)]
        + [pl.BlockSpec(memory_space=pltpu.HBM)] * 6,
        out_shape=(
            jax.ShapeDtypeStruct((rows, clip_cache.shape[1]), jnp.float32),
            jax.ShapeDtypeStruct((len(ids), count), jnp.int32),
            jax.ShapeDtypeStruct((len(ids), count // 2), jnp.int32),
            jax.ShapeDtypeStruct((1, count), jnp.int32),
        ),
        scratch_shapes=[pltpu.VMEM((1, count), jnp.int32)] * 3 + [pltpu.SemaphoreType.DMA((6,))],
        compiler_params=pltpu.CompilerParams(vmem_limit_bytes=60 * 2**20),
        cost_estimate=BRIEF,
        name="layout",
    )(odd, clip_cache, dose_scale, focus_term, *[value.reshape(1, count) for value in ids])


def one_hot(index, first, size):
    positions = first + lax.broadcasted_iota(jnp.int32, (size, index.shape[1]), 0)
    return jnp.where(positions == index, 1.0, 0.0).astype(jnp.bfloat16)


def first_counts_kernel(focus_count, table, ids, *refs):
    outs, copied, sem = refs[:COUNT_PARTS], refs[COUNT_PARTS], refs[COUNT_PARTS + 1]
    copy = pltpu.make_async_copy(table, copied, sem)
    copy.start()
    counts_kernel(focus_count, 0, ids, *outs)
    copy.wait()


def first_counts_of(table, ids, clip_count, dose_count, focus_count):
    settings = dose_count * focus_count
    part = jax.ShapeDtypeStruct((settings // COUNT_PARTS, clip_count), jnp.float32)
    return pl.pallas_call(
        lambda *refs: first_counts_kernel(focus_count, *refs),
        in_specs=[pl.BlockSpec(memory_space=pltpu.HBM), pl.BlockSpec(memory_space=pltpu.VMEM)],
        out_shape=[part] * COUNT_PARTS + [jax.ShapeDtypeStruct(table.shape, table.dtype)],
        scratch_shapes=[pltpu.SemaphoreType.DMA],
        compiler_params=pltpu.CompilerParams(vmem_limit_bytes=VMEM_LIMIT),
        cost_estimate=BRIEF,
        name="counts",
    )(table, ids)


def counts_kernel(focus_count, given, *refs):
    count_refs, id_refs, outs = refs[:given], refs[given : -COUNT_PARTS], refs[-COUNT_PARTS:]
    part, clip_count = outs[0].shape
    settings = part * COUNT_PARTS
    half = clip_count // 2
    chunk = min(2048, id_refs[-1].shape[1])
    total = jnp.zeros((2 * settings, half), jnp.float32)
    for ids in id_refs:
        for start in range(0, ids.shape[1], chunk):
            some = slice(start, start + chunk)
            clip = ids[0:1, some]
            setting = ids[1:2, some] * focus_count + ids[2:3, some]
            upper = clip >= half
            left = one_hot(jnp.where(upper, setting + settings, setting), 0, 2 * settings)
            right = one_hot(jnp.where(upper, clip - half, clip), 0, half)
            total += bdot(left, right, ((1,), (1,)))
    for k, out in enumerate(outs):
        lower = total[k * part : (k + 1) * part]
        upper = total[settings + k * part : settings + (k + 1) * part]
        value = jnp.concatenate([lower, upper], axis=1)
        out[...] = count_refs[k][...] + value if given else value


def counts_of(ids, base, clip_count, dose_count, focus_count):
    settings = dose_count * focus_count
    part = jax.ShapeDtypeStruct((settings // COUNT_PARTS, clip_count), jnp.float32)
    return pl.pallas_call(
        lambda *refs: counts_kernel(focus_count, len(base), *refs),
        out_shape=[part] * COUNT_PARTS,
        compiler_params=pltpu.CompilerParams(vmem_limit_bytes=VMEM_LIMIT),
        cost_estimate=BRIEF,
        name="counts",
    )(*base, *ids)


def prepare_gram(counts, tables, sizes, out, high, low, doses, numbers):
    clip_count, dose_count, focus_count = sizes
    width = out.shape[0]
    panels = len(tables)
    for q, table in enumerate(tables):
        part = slice(q * width, (q + 1) * width)
        high[:, part], low[:, part] = split(table[:clip_count, :])
        doses[:, part] = table[clip_count : clip_count + dose_count, :]
    focuses = jnp.concatenate([table[clip_count + dose_count :, :] for table in tables], axis=1)

    counts_high, counts_low = split(counts)
    totals = (
        bdot(counts_high, high[...]) + bdot(counts_high, low[...]) + bdot(counts_low, high[...])
    )
    mixed = jnp.zeros((focus_count, panels * width), jnp.float32)
    per_focus = jnp.sum(counts, axis=1, keepdims=True)
    number = jnp.zeros((focus_count, 1), jnp.float32)
    for b in range(dose_count):
        some = slice(b * focus_count, (b + 1) * focus_count)
        mixed += totals[some] * doses[b : b + 1, :]
        number += per_focus[some]
        numbers[b : b + 1, :] = jnp.sum(counts[some], axis=0, keepdims=True)
    lefts = jnp.concatenate([focuses[:, :width], mixed[:, :width]], axis=0)
    rights = jnp.concatenate([mixed + number * focuses, focuses], axis=0)
    out[...] = fdot(lefts, rights, ((0,), (0,)))


def add_doses(first, own_doses, begin, group, columns, out, high, low, doses, numbers):
    width = out.shape[0]
    pieces = [first * numbers[pl.ds(begin + k, 1), :] for k in range(group)]
    left_high, left_low = split(jnp.concatenate(pieces, axis=0))
    products = (
        bdot(left_high, high[:, columns])
        + bdot(left_high, low[:, columns])
        + bdot(left_low, high[:, columns])
    )
    lanes = lax.broadcasted_iota(jnp.int32, own_doses.shape, 1)
    total = jnp.zeros_like(out[:, columns])
    for k in range(group):
        column = jnp.sum(jnp.where(lanes == begin + k, own_doses, 0.0), axis=1, keepdims=True)
        row = doses[pl.ds(begin + k, 1), columns]
        total += products[k * width : (k + 1) * width] * column * row
    out[:, columns] += total


def gram_scratch(clip_count, dose_count, total):
    return [
        pltpu.VMEM((clip_count, total), jnp.bfloat16),
        pltpu.VMEM((clip_count, total), jnp.bfloat16),
        pltpu.VMEM((dose_count, total), jnp.float32),
        pltpu.VMEM((dose_count, clip_count), jnp.float32),
    ]


def counts_from(refs):
    own, more = refs[:COUNT_PARTS], refs[COUNT_PARTS:]
    return jnp.concatenate([a[...] + b[...] for a, b in zip(own, more)], axis=0)


def pair_kernel(sizes, *refs):
    counts, refs = refs[: 2 * COUNT_PARTS], refs[2 * COUNT_PARTS :]
    own, partner, out, scratch = refs[0], refs[1], refs[2], refs[3:]
    clip_count, dose_count, _ = sizes
    prepare_gram(counts_from(counts), [own, partner], sizes, out, *scratch)
    first = own[:clip_count, :].T
    own_doses = own[clip_count : clip_count + dose_count, :].T
    group = 8

    def some_doses(step, carry):
        add_doses(first, own_doses, step * group, group, slice(None), out, *scratch)
        return carry

    lax.fori_loop(0, dose_count // group, some_doses, 0)


def pair_gram_of(counts, more, tables, sizes):
    width = tables[0].shape[1]
    return pl.pallas_call(
        lambda *refs: pair_kernel(sizes, *refs),
        out_shape=jax.ShapeDtypeStruct((width, 2 * width), jnp.float32),
        scratch_shapes=gram_scratch(*sizes[:2], 2 * width),
        compiler_params=pltpu.CompilerParams(vmem_limit_bytes=VMEM_LIMIT),
        cost_estimate=BRIEF,
        name="pair_gram",
    )(*counts, *more, *tables)


def quad_kernel(sizes, *refs):
    counts, refs = refs[: 2 * COUNT_PARTS], refs[2 * COUNT_PARTS :]
    tables, earlier, (out, sent, *laid_out) = refs[:4], refs[4], refs[5:]
    clip_count, dose_count, _ = sizes
    width = out.shape[0]
    prepare_gram(counts_from(counts), tables, sizes, out, *laid_out)
    first = tables[0][:clip_count, :].T
    own_doses = tables[0][clip_count : clip_count + dose_count, :].T
    group = 8

    def some_doses(step, carry):
        add_doses(first, own_doses, step * group, group, slice(None), out, *laid_out)
        return carry

    lax.fori_loop(0, dose_count // group, some_doses, 0)
    sent[:, :width] = earlier[:, :width]
    sent[:, width:] = out[:, : 3 * width]


def quad_gram_of(counts, more, tables, earlier, sizes):
    width = tables[0].shape[1]
    clip_count, dose_count, _ = sizes
    square = jax.ShapeDtypeStruct((width, 4 * width), jnp.float32)
    half = jax.ShapeDtypeStruct((clip_count, 4 * width), jnp.bfloat16)
    doses = jax.ShapeDtypeStruct((dose_count, 4 * width), jnp.float32)
    return pl.pallas_call(
        lambda *refs: quad_kernel(sizes, *refs),
        out_shape=(square, square, half, half, doses),
        scratch_shapes=gram_scratch(clip_count, dose_count, 4 * width)[3:],
        compiler_params=pltpu.CompilerParams(vmem_limit_bytes=VMEM_LIMIT),
        cost_estimate=BRIEF,
        name="quad_gram",
    )(*counts, *more, *tables, earlier)


def eye(size):
    rows = lax.broadcasted_iota(jnp.int32, (size, size), 0)
    cols = lax.broadcasted_iota(jnp.int32, (size, size), 1)
    return rows == cols


def diagonal_row(square):
    return jnp.sum(jnp.where(eye(square.shape[0]), square, 0.0), axis=0, keepdims=True)


def column_of(row):
    square = jnp.broadcast_to(row, (row.shape[1], row.shape[1]))
    return jnp.sum(jnp.where(eye(row.shape[1]), square, 0.0), axis=1, keepdims=True)


def inverses(couplings, factors, powers):
    products = [dot6(k, k.T) for k in couplings]
    bound = 0.0
    for product in products:
        rows = jnp.max(jnp.sum(jnp.abs(product), axis=0))
        frobenius = jnp.sqrt(jnp.max(jnp.sum(jnp.sum(product * product, axis=0, keepdims=True), axis=1)))
        bound = jnp.maximum(bound, jnp.minimum(rows, frobenius))
    size = products[0].shape[0]
    identity = jnp.where(eye(size), 1.0, 0.0)
    matrices = [identity + product for product in products]
    start = 2.0 / (2.0 + bound)
    rate = bound / (2.0 + bound)
    for factor, power, matrix in zip(factors, powers, matrices):
        error = identity - start * matrix
        factor[...] = identity + error
        power[...] = dot3(error, error)

    def square(rate):
        for factor, power in zip(factors, powers):
            value, now = power[...], factor[...]
            both = dot3(jnp.concatenate([now, value], axis=0), value)
            factor[...] = now + both[:size]
            power[...] = both[size:]
        return rate * rate

    lax.while_loop(lambda rate: rate > 3e-4, square, rate * rate)
    for factor in factors:
        factor[...] = start * factor[...]

    def correct(step, carry):
        for factor, matrix in zip(factors, matrices):
            guess = factor[...]
            factor[...] = guess + dot3(guess, identity - dot6(matrix, guess))
        return carry

    lax.fori_loop(0, jnp.where(bound > 4.0, 4, 1), correct, 0)
    return [factor[...] for factor in factors]


def weights_kernel(total_rows, odd_ref, pair_ref, own_ref, other_ref, weights, *spaces):
    width = weights.shape[0]
    odd = odd_ref[0] == 1
    sign = jnp.where(odd, -1.0, 1.0).astype(jnp.float32)
    block = lambda ref, j: ref[:, j * width : (j + 1) * width]
    identity = jnp.where(eye(width), 1.0, 0.0)

    diagonals = [
        diagonal_row(block(own_ref, 0)),
        diagonal_row(block(pair_ref, 0)),
        diagonal_row(block(other_ref, 1)),
        diagonal_row(block(other_ref, 0)),
    ]
    scales = [1.0 / jnp.sqrt(d / total_rows + EPSILON) for d in diagonals]
    columns = [column_of(s) for s in scales]
    scaled = lambda value, i, j: value * columns[i] * scales[j]
    squares = [d * s * s for d, s in zip(diagonals, scales)]

    own_a = scaled(block(own_ref, 0), 0, 0)
    own_b = scaled(block(pair_ref, 0), 1, 1)
    other_a = scaled(block(other_ref, 1), 2, 2)
    other_b = scaled(block(other_ref, 0), 3, 3)
    pair_a = scaled(block(own_ref, 3), 0, 2)
    pair_b = scaled(block(pair_ref, 1), 1, 3)
    cross_oo = scaled(block(own_ref, 1), 0, 1)
    cross_op = scaled(block(own_ref, 2), 0, 3)
    cross_po = scaled(block(other_ref, 3), 2, 1)
    cross_pp = scaled(block(other_ref, 2), 2, 3)

    coupling_a = sign * 0.5 * pair_a / (column_of(squares[0]) + squares[2])
    coupling_b = sign * 0.5 * pair_b / (column_of(squares[1]) + squares[3])
    inverse_a, inverse_b = inverses([coupling_a, coupling_b], spaces[:2], spaces[2:])

    def halves(inverse, coupling):
        own_partner = 2.0 * dot6(inverse, coupling)
        first = (2.0 * inverse - identity, -own_partner.T)
        second = (own_partner, identity - dot6(coupling.T, own_partner))
        return first, second

    own_cols_a, other_cols_a = halves(inverse_a, coupling_a)
    own_cols_b, other_cols_b = halves(inverse_b, coupling_b)
    left = [jnp.where(odd, o, p) for o, p in zip(own_cols_a, other_cols_a)]
    right = [jnp.where(odd, p, o) for o, p in zip(own_cols_b, other_cols_b)]
    left = jnp.concatenate(left, axis=0)
    right = jnp.concatenate(right, axis=0)

    def square_of(a, b, c):
        top = jnp.concatenate([a, b], axis=1)
        return jnp.concatenate([top, jnp.concatenate([b.T, c], axis=1)], axis=0)

    gram_a = square_of(own_a, pair_a, other_a)
    gram_b = square_of(own_b, pair_b, other_b)
    cross = jnp.concatenate(
        [
            jnp.concatenate([cross_oo, cross_op], axis=1),
            jnp.concatenate([cross_po, cross_pp], axis=1),
        ],
        axis=0,
    )
    left_squares = jnp.sum(left * dot3(gram_a, left), axis=0, keepdims=True)
    right_squares = jnp.sum(right * dot3(gram_b, right), axis=0, keepdims=True)
    between = dot3(left.T, dot3(cross, right))
    coupling = 0.5 * between / (column_of(left_squares) + right_squares)
    (inverse,) = inverses([coupling], spaces[:1], spaces[2:3])
    first, second = halves(inverse, coupling)
    top = jnp.where(odd, second[0], first[0])
    bottom = jnp.where(odd, second[1], first[1])
    part_a = dot6(left, top)
    part_b = dot6(right, bottom)
    for k, (part, half, column) in enumerate(
        [(part_a, 0, 0), (part_b, 0, 1), (part_b, 1, 3), (part_a, 1, 2)]
    ):
        piece = part[half * width : (half + 1) * width] * columns[column]
        weights[:, k * width : (k + 1) * width] = piece.T


def weights_of(odd, pair_gram, own_gram, other_gram, total_rows):
    width = own_gram.shape[0]
    whole = lambda value: pl.BlockSpec(value.shape, lambda: (0, 0))
    return pl.pallas_call(
        lambda *refs: weights_kernel(total_rows, *refs),
        in_specs=[pl.BlockSpec(memory_space=pltpu.SMEM)]
        + [whole(value) for value in (pair_gram, own_gram, other_gram)],
        out_specs=pl.BlockSpec((width, 4 * width), lambda: (0, 0)),
        out_shape=jax.ShapeDtypeStruct((width, 4 * width), jnp.float32),
        scratch_shapes=[pltpu.VMEM((width, width), jnp.float32)] * 4,
        compiler_params=pltpu.CompilerParams(vmem_limit_bytes=VMEM_LIMIT),
        name="weights",
    )(odd, pair_gram, own_gram, other_gram)


def rotate_kernel(group, piece, start, high, low, doses, weights, pairs, ids, *refs):
    tables, (out, products, left, places, rows, place_sem, out_sems) = refs[:4], refs[4:]
    clip_count, width = high.shape[0], weights.shape[0]
    over_lanes = ((1,), (1,))
    tall = MARGIN
    fetch = pltpu.make_async_copy(pairs, places, place_sem)
    fetch.start()
    focuses = jnp.concatenate([table[start:, :] for table in tables], axis=1)
    focus_count = focuses.shape[0]
    shifts = jnp.concatenate(split(fdot(focuses, weights[...], over_lanes)), axis=0)
    left[...] = jnp.concatenate([high[...], low[...], high[...]], axis=1)

    def some_doses(step, carry):
        scaled = [weights[...] * doses[pl.ds(step * group + k, 1), :] for k in range(group)]
        right_high, right_low = split(jnp.concatenate(scaled, axis=0))
        right = jnp.concatenate([right_high, right_high, right_low], axis=1)
        result = bdot(left[...], right, over_lanes)
        for k in range(group):
            begin = pl.multiple_of((step * group + k) * clip_count + tall, tall)
            products[pl.ds(begin, clip_count), :] = result[:, k * width : (k + 1) * width]
        return carry

    lax.fori_loop(0, doses.shape[0] // group, some_doses, 0)
    fetch.wait()
    unroll = 256
    sublanes = lax.broadcasted_iota(jnp.int32, (tall, width), 0)
    slots = lax.broadcasted_iota(jnp.int32, (2 * focus_count, unroll), 0)
    slots = jnp.where(slots >= focus_count, slots - focus_count, slots)

    def some_rows(part, carry):
        first = pl.multiple_of(part * unroll, unroll)
        hot = jnp.where(slots == ids[2:3, pl.ds(first, unroll)], 1.0, 0.0).astype(jnp.bfloat16)
        moved = bdot(hot, shifts, ((0,), (0,)))
        for begin in range(0, unroll, tall):
            starts = [places[0, first + begin + k] + (tall - k) for k in range(tall)]
            found = [products[pl.ds(start, tall), :] for start in starts]
            tile = found[0]
            for k in range(1, tall):
                tile = jnp.where(sublanes == k, found[k], tile)
            rows[pl.ds(first + begin, tall), :] = tile + moved[begin : begin + tall]
        return carry

    copies = []
    for k in range(rows.shape[0] // piece):
        lax.fori_loop(k * piece // unroll, (k + 1) * piece // unroll, some_rows, 0)
        span = pl.ds(k * piece, piece)
        copies.append(pltpu.make_async_copy(rows.at[span], out.at[span], out_sems.at[k]))
        copies[-1].start()
    for copy in copies:
        copy.wait()


def rotate(high, low, doses, weights, pairs, ids, tables, sizes):
    width = weights.shape[0]
    clip_count, dose_count, _ = sizes
    count = pairs.shape[1]
    piece = min(1024, count)
    vmem = pl.BlockSpec(memory_space=pltpu.VMEM)
    return pl.pallas_call(
        lambda *refs: rotate_kernel(8, piece, clip_count + dose_count, *refs),
        in_specs=[vmem] * 4 + [pl.BlockSpec(memory_space=pl.ANY)] + [vmem] * 5,
        out_specs=pl.BlockSpec(memory_space=pltpu.HBM),
        out_shape=jax.ShapeDtypeStruct((count, width), jnp.float32),
        scratch_shapes=[
            pltpu.VMEM((dose_count * clip_count + 2 * MARGIN, width), jnp.float32),
            pltpu.VMEM((clip_count, 3 * high.shape[1]), jnp.bfloat16),
            pltpu.SMEM((1, count), jnp.int32),
            pltpu.VMEM((count, width), jnp.float32),
            pltpu.SemaphoreType.DMA,
            pltpu.SemaphoreType.DMA((count // piece,)),
        ],
        compiler_params=pltpu.CompilerParams(vmem_limit_bytes=VMEM_LIMIT),
        name="rotate",
    )(high, low, doses, weights, pairs, ids, *tables)


def shards(clip_cache, dose_scale, focus_term, clip_ids, dose_ids, focus_ids):
    row_count = clip_ids.shape[0]
    slabs = lax.axis_size("slab")
    clip_count, width = clip_cache.shape
    dose_count, focus_count = dose_scale.shape[0], focus_term.shape[0]
    odd = (lax.axis_index("panel") % 2).astype(jnp.int32)

    table_b, ids, own_ids, pairs = layout(
        odd.reshape(1), clip_cache, dose_scale, focus_term, clip_ids, dose_ids, focus_ids
    )
    table_a = from_previous_pair(table_b)
    others = from_other_slabs(own_ids)
    table_d = from_partner(table_b)
    sizes = (clip_count, dose_count, focus_count)
    *counts, table_b = first_counts_of(table_b, own_ids, *sizes)
    table_d, others = lax.optimization_barrier((table_d, others))
    counts = counts_of(others, counts, *sizes)
    more = [from_partner(part) for part in counts]
    table_a, more = lax.optimization_barrier((table_a, more))
    table_c = from_partner(table_a)
    pair_gram = pair_gram_of(counts, more, [table_b, table_d], sizes)
    table_c, pair_gram = lax.optimization_barrier((table_c, pair_gram))
    tables = [table_a, table_b, table_d, table_c]
    own_gram, sent, high, low, doses = quad_gram_of(counts, more, tables, pair_gram, sizes)
    other_gram = from_partner(sent)
    weights = weights_of(odd.reshape(1), pair_gram, own_gram, other_gram, row_count * slabs)
    return rotate(high, low, doses, weights, pairs, ids, tables, sizes)


def solution(mesh):
    return jax.shard_map(
        shards,
        mesh=mesh,
        in_specs=(
            P(None, "panel"),
            P(None, "panel"),
            P(None, "panel"),
            P("slab"),
            P("slab"),
            P("slab"),
        ),
        out_specs=P("slab", "panel"),
        check_vma=False,
    )
```

time: 408 us -> 62.1 us (0.15); the launches traced: 402 us -> 62.6 us
  waiting for transfers between devices: 131 us -> 4.63 us
  other arithmetic: 115 us -> 0 us
  matrix products: 75.7 us -> 0 us
  Pallas kernels: 0 us -> 47.2 us
  local copies, waits for them, and re-layouts: 49 us -> 1.89 us
  between operations: 16.7 us -> 0.25 us
  blocking collectives: 13.4 us -> 0 us
  starting transfers between devices: 0.57 us -> 8.61 us
    another operation x19 -> x0, other arithmetic: 109 us -> none  [the longest x14 69.2 us: block_rotation(): factor = jnp.linalg.cholesky(symmetric)]
    dot_general x10 -> x0, matrix products: 71.4 us -> none  [the longest x2 31 us: slab_gram(): lax.dot_general(pair_block, pair_block, (((0,), (0,)), ((), ())), precisi...]
    psum x2 -> x0, waiting for transfers between devices: 67.5 us -> none  [slab_gram(): return lax.psum(gram_local, 'slab')]
    ppermute x3 -> x9, waiting for transfers between devices: 63.6 us -> 4.63 us  [the longest x5 2.35 us: from_partner(): return lax.ppermute(value, 'panel', [(i, i ^ 1) for i in range(count)])]
    pallas_call x0 -> x7, Pallas kernels: none -> 47.2 us  [the longest x1 17.6 us: rotate(): pl.pallas_call(lambda *refs: rotate_kernel(8, piece, clip_count + dose_co...]
    gather x4 -> x0, local copies, waits for them, and re-layouts: 38.9 us -> none  [the longest x2 33.6 us: shards(): jacobian = jnp.take(clip_cache, clip_ids, axis=0) * dose_part + focus_part]
    psum x1 -> x0, blocking collectives: 13.4 us -> none  [shards(): col_squares = lax.psum(jnp.sum(jacobian * jacobian, axis=0), 'slab')]
    ppermute x3 -> x9, starting transfers between devices: 0.06 us -> 8.61 us  [the longest x3 4.39 us: from_other_slabs(): lax.ppermute(value, 'slab', [(i, target(i, d)) for i in range(slabs)])]
  transfers between devices with their start and end apart: 5 -> 9, of which waited for: 5 -> 5; matrix products, arithmetic and copies ran while one was open for 0% -> 0% of each run, Pallas kernels for 0% -> 15%
where the time goes in v1:
time: 62.1 us; the launch traced here: 62.6 us
  Pallas kernels  47.2 us (76%)
  starting transfers between devices  8.61 us (14%)
  waiting for transfers between devices  4.63 us (7%)
  local copies, waits for them, and re-layouts  1.89 us (3%)
    pallas_call x1, Pallas kernels, rotate(): pl.pallas_call(lambda *refs: rotate_kernel(8, piece, clip_count + dose_co...  17.6 us
    pallas_call x1, Pallas kernels, weights_of(): pl.pallas_call(lambda *refs: weights_kernel(total_rows, *refs), in_specs=...  9.66 us
    pallas_call x1, Pallas kernels, quad_gram_of(): pl.pallas_call(lambda *refs: quad_kernel(sizes, *refs), out_shape=(square...  8.55 us
    pallas_call x1, Pallas kernels, pair_gram_of(): pl.pallas_call(lambda *refs: pair_kernel(sizes, *refs), out_shape=jax.Sha...  4.71 us
    ppermute x3, starting transfers between devices, from_other_slabs(): lax.ppermute(value, 'slab', [(i, target(i, d)) for i in range(slabs)])  4.39 us
    pallas_call x1, Pallas kernels, counts_of(): pl.pallas_call(lambda *refs: counts_kernel(focus_count, len(base), *refs)...  3.45 us
    ppermute x1, starting transfers between devices, from_previous_pair(): lax.ppermute(value, 'panel', [(i, (i + 2) % count) for i in range(count)])  2.55 us
    ppermute x5, waiting for transfers between devices, from_partner(): return lax.ppermute(value, 'panel', [(i, i ^ 1) for i in range(count)])  2.35 us
  transfers between devices with their start and end apart: 9, of which 5 were waited for; matrix products, arithmetic and copies ran while one was open for 0% of the time, Pallas kernels for 15%

profile of v1, /device:TPU:0, one launch (start us, length us, event | category | flops | bytes accessed | tf_op | source)
XLA Modules:
  0.0 62.6 jit_solution(10311424745746693957)
XLA Ops:
  0.0 1.9 %layout.1 = (f32[1048,128]{1,0:T(8,128)}, s32[3,8192]{1,0:T(4,128)}, s32[3,4096]{1,0:T(4,128)}, s32[1,8192]{1,0:T(1,128)}) custom-call(s32[1]{0:T(128)} %bitcast.odd_ref.refs_0_, f32[1024,128]{1,0:T(8,128)} %clips.1, f32[16,128]{1,0:T(8,128)} %doses.1, f32[8,128]{1,0:T(8,128)} %focuses.1, s32[1,8192]{1,0:T(1,128)} %bitcast.4, s32[1,8192]{1,0:T(1,128)} %bitcast.5, ...), custom_call_target="tpu_custom_call" | custom-call | flops 1 | bytes 1 | tf_op jit(solution)/shard_map/layout/pallas_call | solution.py:96
  2.0 0.5 collective-permute-start
  2.5 2.6 %collective-permute-start.4 = (f32[1048,128]{1,0:T(8,128)}, f32[1048,128]{1,0:T(8,128)S(1)}, u32[]{:S(2)}, u32[]{:S(2)}) collective-permute-start(f32[1048,128]{1,0:T(8,128)} %get-tuple-element.28.refs_0_), channel_id=1, source_target_pairs={{0,8},{4,12},{8,16},{12,20},{16,24},{20,28},{24,0},{28,4},{1,9},{5... | collective-permute-start | bytes 1609736 | tf_op jit(solution)/shard_map/ppermute | solution.py:23
  5.0 3.6 %collective-permute-start.3 = (s32[3,4096]{1,0:T(4,128)}, s32[3,4096]{1,0:T(4,128)S(1)}, u32[]{:S(2)}, u32[]{:S(2)}) collective-permute-start(s32[3,4096]{1,0:T(4,128)} %get-tuple-element.29.refs_1_), channel_id=1, source_target_pairs={{0,3},{1,2},{2,1},{3,0},{4,7},{5,6},{6,5},{7,4},{8,11},{9,10},{10,... | collective-permute-start | bytes 147464 | tf_op jit(solution)/shard_map/ppermute | solution.py:31
  8.6 0.0 collective-permute-start.2
  8.6 0.8 %collective-permute-start.1 = (s32[3,4096]{1,0:T(4,128)}, s32[3,4096]{1,0:T(4,128)S(1)}, u32[]{:S(2)}, u32[]{:S(2)}) collective-permute-start(s32[3,4096]{1,0:T(4,128)} %get-tuple-element.29.refs_1_), channel_id=1, source_target_pairs={{0,1},{1,0},{2,3},{3,2},{4,5},{5,4},{6,7},{7,6},{8,9},{9,8},{10,11... | collective-permute-start | bytes 147464 | tf_op jit(solution)/shard_map/ppermute | solution.py:31
  9.4 1.0 %copy-done = f32[1048,128]{1,0:T(8,128)S(1)} copy-done((f32[1048,128]{1,0:T(8,128)S(1)}, f32[1048,128]{1,0:T(8,128)}, u32[]{:S(2)}) %copy-start) | copy-done | bytes 536600
  10.5 0.8 %copy-done.2 = s32[3,4096]{1,0:T(4,128)S(1)} copy-done((s32[3,4096]{1,0:T(4,128)S(1)}, s32[3,4096]{1,0:T(4,128)}, u32[]{:S(2)}) %copy-start.2) | copy-done | bytes 49176
  11.3 1.3 %counts.2 = (f32[64,1024]{1,0:T(8,128)S(1)}, f32[64,1024]{1,0:T(8,128)S(1)}, f32[1048,128]{1,0:T(8,128)S(1)}) custom-call(f32[1048,128]{1,0:T(8,128)S(1)} %copy-done, s32[3,4096]{1,0:T(4,128)S(1)} %copy-done.2), custom_call_target="tpu_custom_call" | custom-call | flops 1 | bytes 1 | tf_op jit(solution)/shard_map/counts/pallas_call | solution.py:129
  12.7 0.0 collective-permute-done.3.refs_4_
  12.7 2.1 %collective-permute-done.2.refs_3_ = s32[3,4096]{1,0:T(4,128)S(1)} collective-permute-done((s32[3,4096]{1,0:T(4,128)}, s32[3,4096]{1,0:T(4,128)S(1)}, u32[]{:S(2)}, u32[]{:S(2)}) %collective-permute-start.2) | collective-permute-done | bytes 49184 | tf_op jit(solution)/shard_map/ppermute | solution.py:31
  14.7 3.4 %counts.3 = (f32[64,1024]{1,0:T(8,128)S(1)}, f32[64,1024]{1,0:T(8,128)S(1)}) custom-call(f32[64,1024]{1,0:T(8,128)S(1)} %get-tuple-element.30.refs_0_, f32[64,1024]{1,0:T(8,128)S(1)} %get-tuple-element.31.refs_1_, s32[3,4096]{1,0:T(4,128)S(1)} %collective-permute-done.1.refs_2_, s32[3,4096]{1,0:T(4,128)S(1)} %collective-permute-done.2.refs_3_, ...), custom_call_target="tpu_custom_call" | custom-call | flops 1 | bytes 1 | tf_op jit(solution)/shard_map/counts/pallas_call | solution.py:166
  18.2 0.1 collective-permute-start.5
  18.3 0.5 collective-permute-start.6
  18.8 0.2 collective-permute-done.4.refs_4_.refs_6_
  19.0 0.8 %collective-permute-done.5.refs_2_ = f32[64,1024]{1,0:T(8,128)S(1)} collective-permute-done((f32[64,1024]{1,0:T(8,128)S(1)}, f32[64,1024]{1,0:T(8,128)S(1)}, u32[]{:S(2)}, u32[]{:S(2)}) %collective-permute-start.5) | collective-permute-done | bytes 262176 | tf_op jit(solution)/shard_map/ppermute | solution.py:18
  19.8 0.4 collective-permute-done.6.refs_3_
  20.2 0.1 collective-permute-start.7
  20.3 4.7 %pair_gram.1.refs_8_.refs_1_ = f32[128,256]{1,0:T(8,128)S(1)} custom-call(f32[64,1024]{1,0:T(8,128)S(1)} %get-tuple-element.35.refs_0_, f32[64,1024]{1,0:T(8,128)S(1)} %get-tuple-element.36.refs_1_, f32[64,1024]{1,0:T(8,128)S(1)} %collective-permute-done.5.refs_2_, f32[64,1024]{1,0:T(8,128)S(1)} %collective-permute-done.6.refs_3_, ...), custom_call_target="tpu_custom_call" | custom-call | flops 1 | bytes 1 | tf_op jit(solution)/shard_map/pair_gram/pallas_call | solution.py:252
  25.0 8.5 %quad_gram.1 = (f32[128,512]{1,0:T(8,128)S(1)}, f32[128,512]{1,0:T(8,128)S(1)}, bf16[1024,512]{1,0:T(8,128)(2,1)S(1)}, bf16[1024,512]{1,0:T(8,128)(2,1)S(1)}, f32[16,512]{1,0:T(8,128)S(1)}) custom-call(f32[64,1024]{1,0:T(8,128)S(1)} %get-tuple-element.35.refs_0_, f32[64,1024]{1,0:T(8,128)S(1)} %get-tuple-element.36.refs_1_, ...), custom_call_target="tpu_custom_call" | custom-call | flops 1 | bytes 1 | tf_op jit(solution)/shard_map/quad_gram/pallas_call | solution.py:287
  33.6 0.4 collective-permute-start.8
  34.0 1.2 %collective-permute-done.8.refs_3_ = f32[128,512]{1,0:T(8,128)S(1)} collective-permute-done((f32[128,512]{1,0:T(8,128)S(1)}, f32[128,512]{1,0:T(8,128)S(1)}, u32[]{:S(2)}, u32[]{:S(2)}) %collective-permute-start.8) | collective-permute-done | bytes 262176 | tf_op jit(solution)/shard_map/ppermute | solution.py:18
  35.2 9.7 %weights.1.refs_3_ = f32[128,512]{1,0:T(8,128)S(1)} custom-call(s32[1]{0:T(128)} %bitcast.odd_ref.refs_0_, f32[128,256]{1,0:T(8,128)S(1)} %pair_gram.1.refs_8_.refs_1_, f32[128,512]{1,0:T(8,128)S(1)} %get-tuple-element.47.refs_2_, f32[128,512]{1,0:T(8,128)S(1)} %collective-permute-done.8.refs_3_), custom_call_target="tpu_custom_call" | custom-call | tf_op jit(solution)/shard_map/weights/pallas_call | solution.py:430
  44.9 17.6 %rotate.1 = f32[8192,128]{1,0:T(8,128)} custom-call(bf16[1024,512]{1,0:T(8,128)(2,1)S(1)} %get-tuple-element.44.refs_0_, bf16[1024,512]{1,0:T(8,128)(2,1)S(1)} %get-tuple-element.45.refs_1_, f32[16,512]{1,0:T(8,128)S(1)} %get-tuple-element.46.refs_2_, f32[128,512]{1,0:T(8,128)S(1)} %weights.1.refs_3_, s32[1,8192]{1,0:T(1,128)S(1)} %copy-done.3, ...), custom_call_target="tpu_custom_call" | custom-call | tf_op jit(solution)/shard_map/rotate/pallas_call | solution.py:500
  (9 shorter events, 0.0 us)
Async XLA Ops:
  2.0 12.8 %collective-permute-start = (f32[1048,128]{1,0:T(8,128)}, f32[1048,128]{1,0:T(8,128)S(1)}, u32[]{:S(2)}, u32[]{:S(2)}) collective-permute-start(f32[1048,128]{1,0:T(8,128)} %get-tuple-element.28.refs_0_), channel_id=1, source_target_pairs={{0,4},{4,0},{8,12},{12,8},{16,20},{20,16},{24,28},{28,24},{1,5},{5... | collective-permute-start | bytes 1609736 | tf_op jit(solution)/shard_map/ppermute | solution.py:18
  2.5 16.5 %collective-permute-start.4 = (f32[1048,128]{1,0:T(8,128)}, f32[1048,128]{1,0:T(8,128)S(1)}, u32[]{:S(2)}, u32[]{:S(2)}) collective-permute-start(f32[1048,128]{1,0:T(8,128)} %get-tuple-element.28.refs_0_), channel_id=1, source_target_pairs={{0,8},{4,12},{8,16},{12,20},{16,24},{20,28},{24,0},{28,4},{1,9},{5... | collective-permute-start | bytes 1609736 | tf_op jit(solution)/shard_map/ppermute | solution.py:23
  5.0 7.6 %collective-permute-start.3 = (s32[3,4096]{1,0:T(4,128)}, s32[3,4096]{1,0:T(4,128)S(1)}, u32[]{:S(2)}, u32[]{:S(2)}) collective-permute-start(s32[3,4096]{1,0:T(4,128)} %get-tuple-element.29.refs_1_), channel_id=1, source_target_pairs={{0,3},{1,2},{2,1},{3,0},{4,7},{5,6},{6,5},{7,4},{8,11},{9,10},{10,... | collective-permute-start | bytes 147464 | tf_op jit(solution)/shard_map/ppermute | solution.py:31
  8.6 6.1 %collective-permute-start.2 = (s32[3,4096]{1,0:T(4,128)}, s32[3,4096]{1,0:T(4,128)S(1)}, u32[]{:S(2)}, u32[]{:S(2)}) collective-permute-start(s32[3,4096]{1,0:T(4,128)} %get-tuple-element.29.refs_1_), channel_id=1, source_target_pairs={{0,2},{1,3},{2,0},{3,1},{4,6},{5,7},{6,4},{7,5},{8,10},{9,11},{10,... | collective-permute-start | bytes 147464 | tf_op jit(solution)/shard_map/ppermute | solution.py:31
  8.6 6.1 %collective-permute-start.1 = (s32[3,4096]{1,0:T(4,128)}, s32[3,4096]{1,0:T(4,128)S(1)}, u32[]{:S(2)}, u32[]{:S(2)}) collective-permute-start(s32[3,4096]{1,0:T(4,128)} %get-tuple-element.29.refs_1_), channel_id=1, source_target_pairs={{0,1},{1,0},{2,3},{3,2},{4,5},{5,4},{6,7},{7,6},{8,9},{9,8},{10,11... | collective-permute-start | bytes 147464 | tf_op jit(solution)/shard_map/ppermute | solution.py:31
  9.4 1.0 %copy-start = (f32[1048,128]{1,0:T(8,128)S(1)}, f32[1048,128]{1,0:T(8,128)}, u32[]{:S(2)}) copy-start(f32[1048,128]{1,0:T(8,128)} %get-tuple-element.28.refs_0_) | copy-start | bytes 1609732
  10.5 0.8 %copy-start.2 = (s32[3,4096]{1,0:T(4,128)S(1)}, s32[3,4096]{1,0:T(4,128)}, u32[]{:S(2)}) copy-start(s32[3,4096]{1,0:T(4,128)} %get-tuple-element.29.refs_1_) | copy-start | bytes 147460
  11.3 33.6 %copy-start.1 = (s32[3,8192]{1,0:T(4,128)S(1)}, s32[3,8192]{1,0:T(4,128)}, u32[]{:S(2)}) copy-start(s32[3,8192]{1,0:T(4,128)} %get-tuple-element.50.refs_5_) | copy-start | bytes 294916
  11.3 33.6 %copy-start.3 = (s32[1,8192]{1,0:T(1,128)S(1)}, s32[1,8192]{1,0:T(1,128)}, u32[]{:S(2)}) copy-start(s32[1,8192]{1,0:T(1,128)} %get-tuple-element.49.refs_4_) | copy-start | bytes 98308
  18.2 1.6 %collective-permute-start.5 = (f32[64,1024]{1,0:T(8,128)S(1)}, f32[64,1024]{1,0:T(8,128)S(1)}, u32[]{:S(2)}, u32[]{:S(2)}) collective-permute-start(f32[64,1024]{1,0:T(8,128)S(1)} %get-tuple-element.35.refs_0_), channel_id=1, source_target_pairs={{0,4},{4,0},{8,12},{12,8},{16,20},{20,16},{24,28},{28,24},{1,5},{5... | collective-permute-start | bytes 786440 | tf_op jit(solution)/shard_map/ppermute | solution.py:18
  18.3 1.9 %collective-permute-start.6 = (f32[64,1024]{1,0:T(8,128)S(1)}, f32[64,1024]{1,0:T(8,128)S(1)}, u32[]{:S(2)}, u32[]{:S(2)}) collective-permute-start(f32[64,1024]{1,0:T(8,128)S(1)} %get-tuple-element.36.refs_1_), channel_id=1, source_target_pairs={{0,4},{4,0},{8,12},{12,8},{16,20},{20,16},{24,28},{28,24},{1,5},{5... | collective-permute-start | bytes 786440 | tf_op jit(solution)/shard_map/ppermute | solution.py:18
  20.2 4.9 %collective-permute-start.7 = (f32[1048,128]{1,0:T(8,128)S(1)}, f32[1048,128]{1,0:T(8,128)S(1)}, u32[]{:S(2)}, u32[]{:S(2)}) collective-permute-start(f32[1048,128]{1,0:T(8,128)S(1)} %collective-permute-done.4.refs_4_.refs_6_), channel_id=1, source_target_pairs={{0,4},{4,0},{8,12},{12,8},{16,20},{20,16},{24,28},{28,24},{1,5},{5... | collective-permute-start | bytes 1609736 | tf_op jit(solution)/shard_map/ppermute | solution.py:18
  33.6 1.6 %collective-permute-start.8 = (f32[128,512]{1,0:T(8,128)S(1)}, f32[128,512]{1,0:T(8,128)S(1)}, u32[]{:S(2)}, u32[]{:S(2)}) collective-permute-start(f32[128,512]{1,0:T(8,128)S(1)} %get-tuple-element.48), channel_id=1, source_target_pairs={{0,4},{4,0},{8,12},{12,8},{16,20},{20,16},{24,28},{28,24},{1,5},{5... | collective-permute-start | bytes 786440 | tf_op jit(solution)/shard_map/ppermute | solution.py:18
